TPU v7x, 32 devices: a whole 2x2x4 slice. The times are simulated.
32 devices in a mesh: obs: 4 (over y, x), tm: 8 (over z, core).
Axes of the slice: x: 2, y: 2, z: 4, core: 2. Of those that a mesh axis runs over, the one named last changes fastest.
Arguments:
- flow: float32 [5, 512, 2048], P(None, 'tm', 'obs'), may hold values from -6 to 6
- point_pos: float32 [3, 2048], P(None, 'obs'), may hold values from -1 to 1
- area_vec: float32 [3, 2048], P(None, 'obs'), may hold values from -6.363961 to 6.363961
- observer_angles: float32 [2, 512], P(None, 'obs'), may hold values from -3.140625 to 3.140625
- band_offset: int32 [4, 4], replicated, may hold values from 0 to 61, as said below
Outputs:
- pressure: float32 [512, 512], P('tm', 'obs')
Inputs may be any that keep to these rules, and one draw needn't show every extreme that they name: band_offset[g, b] is the whole number of time steps added to every delay from point block b to observer group g; both 0 and 61 occur.
All inputs are finite; a program needn't handle non-finite values.
Results may differ from a plain program's by a relative error of at most 0.0041.
Values may be sent and summed in bfloat16 or wider, within the bound.
A program may use at most 64 MiB of HBM per device.

v0:
```python
import math

import jax
import jax.numpy as jnp
from jax import lax
from jax.sharding import PartitionSpec as P

LAGS = 4


FOUR_PI_INV = 1.0 / (4.0 * math.pi)
NEAR_RANGE = 3.25
SOUND_STEP = 1.17
SPHERE_RADIUS = 5.0


def extended(block, sides, width):
    for axis, dim in sides:
        count = lax.axis_size(axis)
        forward = [(i, i + 1) for i in range(count - 1)]
        backward = [(target, source) for source, target in forward]
        low = lax.ppermute(
            lax.slice_in_dim(block, block.shape[dim] - width, None, axis=dim), axis, forward
        )
        high = lax.ppermute(lax.slice_in_dim(block, 0, width, axis=dim), axis, backward)
        block = jnp.concatenate([low, block, high], axis=dim)
    return block


def from_behind(block, axis, distance):
    devices = range(lax.axis_size(axis))
    route = [((i - distance) % len(devices), i) for i in devices]
    return lax.ppermute(block, axis, route)


def passed_along(block, axis, distance):
    devices = range(lax.axis_size(axis))
    route = [(i - distance, i) for i in devices if i - distance in devices]
    return lax.ppermute(block, axis, route)


def observer_xyz(angles):
    azimuth = angles[0]
    elevation = angles[1]
    return SPHERE_RADIUS * jnp.stack(
        [
            jnp.cos(azimuth) * jnp.cos(elevation),
            jnp.sin(azimuth) * jnp.cos(elevation),
            jnp.sin(elevation),
        ]
    )


def source_terms(rimmed, area_vec):
    density = 1.0 + 0.2 * rimmed[0]
    velocity = 0.4 * rimmed[1:4]
    pressure = rimmed[4]
    normal_flux = jnp.sum(velocity * area_vec[:, None, :], axis=0)
    mass_flux = density * normal_flux
    loading = pressure[None] * area_vec[:, None, :] + density[None] * velocity * normal_flux[None]
    stacked = jnp.concatenate([mass_flux[None], loading], axis=0)
    rate_terms = 0.5 * (stacked[:, 2:] - stacked[:, :-2])
    return jnp.concatenate([rate_terms, loading[:, 1:-1]], axis=0).astype(jnp.bfloat16)


def pair_weights(observers, points, lag_count):
    separation = observers[:, None, :] - points[:, :, None]
    distance = jnp.sqrt(jnp.sum(separation * separation, axis=0))
    inverse = 1.0 / distance
    direction = separation * inverse[None]
    lag_steps = (distance - NEAR_RANGE) / SOUND_STEP
    shifts = jnp.arange(lag_count).astype(distance.dtype)
    tent_weights = jnp.maximum(0.0, 1.0 - jnp.abs(shifts[None, :, None] - lag_steps[:, None, :]))
    coeffs = (
        jnp.concatenate(
            [
                inverse[None],
                direction * (inverse / SOUND_STEP)[None],
                direction * (inverse * inverse)[None],
            ],
            axis=0,
        )
        * FOUR_PI_INV
    )
    return (coeffs[:, :, None, :] * tent_weights[None]).astype(jnp.bfloat16)


def placed(shard_terms, weights, offset, buffer_len):
    product = jnp.einsum("kts,kswo->two", shard_terms, weights, preferred_element_type=jnp.float32)
    lag_count = product.shape[1]
    combined = jnp.pad(product[:, 0], ((0, lag_count - 1), (0, 0)))
    for lag_index in range(1, lag_count):
        combined = combined + jnp.pad(
            product[:, lag_index], ((lag_index, lag_count - 1 - lag_index), (0, 0))
        )
    canvas = jnp.zeros((buffer_len, product.shape[2]), jnp.float32)
    return lax.dynamic_update_slice(canvas, combined, (offset, jnp.zeros((), jnp.int32)))


def local(flow, point_pos, area_vec, observer_angles, band_offset):
    rimmed = extended(flow, (("tm", 1),), 1)
    terms = source_terms(rimmed, area_vec)
    block_steps = terms.shape[1]
    buffer_len = 2 * block_steps
    group_size = observer_angles.shape[1]
    own_block = lax.axis_index("obs")
    group_places = observer_xyz(observer_angles)
    delays = lax.dynamic_index_in_dim(band_offset, own_block, 0, keepdims=False)
    every_point = lax.all_gather(point_pos, "obs", axis=1, tiled=True)
    block_points = point_pos.shape[1]
    block_total = lax.axis_size("obs")

    def add_block(accumulated, held_terms, turn_index):
        block_index = (own_block - turn_index) % block_total
        shard_points = lax.dynamic_slice_in_dim(
            every_point, block_index * block_points, block_points, 1
        )
        weights = pair_weights(group_places, shard_points, LAGS)
        return accumulated + placed(held_terms, weights, delays[block_index], buffer_len)

    def turn(state, turn_index):
        accumulated, held_terms = state
        accumulated = add_block(accumulated, held_terms, turn_index)
        held_terms = from_behind(held_terms, "obs", 1)
        return ((accumulated, held_terms), None)

    initial = jnp.zeros((buffer_len, group_size), jnp.float32)
    (accumulated, held_terms), unused = lax.scan(
        turn, (initial, terms), jnp.arange(block_total - 1, dtype=jnp.int32)
    )
    summed = add_block(accumulated, held_terms, jnp.int32(block_total - 1))
    carried = passed_along(summed[block_steps:], "tm", 1)
    return summed[:block_steps] + carried


def solution(mesh):
    in_specs = (P(None, "tm", "obs"), P(None, "obs"), P(None, "obs"), P(None, "obs"), P())
    out_specs = P("tm", "obs")
    return jax.shard_map(local, mesh=mesh, in_specs=in_specs, out_specs=out_specs, check_vma=False)
```

profile of v0, /device:TPU:1, one launch (start us, length us, event | category | flops | bytes accessed | tf_op | source)
XLA Modules:
  0.0 65.2 jit_solution(16877035267445873950)
XLA Ops:
  0.0 0.9 %fusion.23 = (f32[5,1,512]{2,1,0:T(1,128)S(1)}, f32[5,1,512]{2,1,0:T(1,128)S(1)}) fusion(f32[5,64,512]{2,1,0:T(8,128)} %param.7), kind=kLoop, calls=%fused_computation.74 | loop fusion | bytes 40960 | tf_op jit(solution)/shard_map/slice | solution.py:23
  0.9 2.0 %collective-permute-start.2 = (f32[5,1,512]{2,1,0:T(1,128)S(1)}, f32[5,1,512]{2,1,0:T(1,128)S(1)}, u32[]{:S(2)}, u32[]{:S(2)}) collective-permute-start(f32[5,1,512]{2,1,0:T(1,128)S(1)} %get-tuple-element.143), channel_id=1, source_target_pairs={{1,0},{2,1},{3,2},{4,3},{5,4},{6,5},{7,6},{9,8},{10,9},{11,10},{12... | collective-permute-start | bytes 30728 | tf_op jit(solution)/shard_map/ppermute | solution.py:25
  2.9 4.5 %collective-permute-start.1 = (f32[5,1,512]{2,1,0:T(1,128)S(1)}, f32[5,1,512]{2,1,0:T(1,128)S(1)}, u32[]{:S(2)}, u32[]{:S(2)}) collective-permute-start(f32[5,1,512]{2,1,0:T(1,128)S(1)} %get-tuple-element.142), channel_id=1, source_target_pairs={{0,1},{1,2},{2,3},{3,4},{4,5},{5,6},{6,7},{8,9},{9,10},{10,11},{11... | collective-permute-start | bytes 30728 | tf_op jit(solution)/shard_map/ppermute | solution.py:22
  7.5 0.7 %broadcast_multiply_fusion.2 = f32[3,512]{1,0:T(4,128)S(1)} fusion(f32[3,512]{1,0:T(4,128)} %param.9), kind=kLoop, calls=%fused_computation.62 | loop fusion | flops 1536 | bytes 12288 | tf_op jit(solution)/shard_map/mul | solution.py:58
  8.2 0.8 %cosine_multiply_fusion = (f32[1,128]{1,0:T(1,128)S(1)}, f32[1,128]{1,0:T(1,128)S(1)}, f32[1,128]{1,0:T(1,128)S(1)}) fusion(f32[2,128]{1,0:T(2,128)} %param.10), kind=kLoop, calls=%fused_computation.69 | loop fusion | flops 256 | bytes 2560 | tf_op jit(solution)/shard_map/mul | solution.py:47
  9.0 6.6 %all_gather.3 = f32[3,2048]{1,0:T(4,128)S(1)} all-gather(f32[3,512]{1,0:T(4,128)} %param.8), channel_id=1, replica_groups=mesh['obs'=4,'tm'=8] {'obs'}, dimensions={1}, use_global_device_ids=true | all-gather | bytes 30720 | tf_op jit(solution)/shard_map/all_gather | solution.py:109
  15.6 0.3 fusion.14
  15.9 0.1 rsqrt_bitcast_fusion.1
  16.0 1.2 %subtract_maximum_fusion.1 = f32[512,4,128]{2,0,1:T(8,128)} fusion(f32[512,128]{1,0:T(8,128)S(1)} %get-tuple-element.149, f32[4]{0:T(128)S(1)} %iota_convert_fusion.1), kind=kLoop, calls=%fused_computation.34 | loop fusion | flops 1048576 | bytes 1310736 | tf_op jit(solution)/shard_map/max | solution.py:73
  17.2 0.3 fusion.13
  17.5 0.2 maximum_multiply_fusion.1
  17.7 0.5 copy-done.2
  18.1 0.6 dynamic_slice.30
  20.6 0.1 pad_maximum_fusion
  21.2 33.1 %while.18 = (s32[]{:T(128)}, f32[128,128]{1,0:T(8,128)S(1)}, bf16[7,64,512]{2,1,0:T(8,128)(2,1)S(1)}, s32[3]{0:T(128)S(1)}, s32[]{:T(128)}, /*index=5*/s32[4]{0:...) while((s32[]{:T(128)}, f32[128,128]{1,0:T(8,128)S(1)}, ...), condition=%wide.region_3.4_spmd, body=%wide.region_1.3_spmd.sunk | while | flops 242583056 | bytes 15959524 | solution.py:128
  21.2 0.8 %collective-permute-start = (bf16[7,64,512]{2,1,0:T(8,128)(2,1)S(1)}, bf16[7,64,512]{2,1,0:T(8,128)(2,1)S(1)}, u32[]{:S(2)}, u32[]{:S(2)}) collective-permute-start(bf16[7,64,512]{2,1,0:T(8,128)(2,1)S(1)} %copy.14), channel_id=1, source_target_pairs={{24,0},{0,8},{8,16},{16,24},{25,1},{1,9},{9,17},{17,25},{26,2},{2,... | collective-permute-start | bytes 1376264 | tf_op jit(solution)/shard_map/while/body/eval_jaxpr/ppermute | solution.py:33
  22.1 0.6 dynamic_slice.41
  23.4 0.3 fusion.29
  23.8 0.2 subtract_maximum_fusion.3
  24.0 0.3 fusion.30
  24.2 0.2 maximum_multiply_fusion.5
  24.4 0.7 %fusion.31 = f32[64,4,128]{2,0,1:T(8,128)S(1)} fusion(f32[512,4,128]{2,0,1:T(8,128)S(1)} %subtract_maximum_fusion.3, f32[7,512,128]{2,1,0:T(8,128)S(1)} %maximum_multiply_fusion.5, bf16[7,64,512]{2,1,0:T(8,128)(2,1)S(1)} %copy.14), kind=kOutput, calls=%fused_computation.5.clone.1 | convolution fusion | flops 238551040 | bytes 3473408 | tf_op jit(solution)/shard_map/while/body/eval_jaxpr/kts,kswo->two/dot_general | solution.py:89
  25.2 0.6 dynamic_slice.42
  27.7 0.4 add.173
  28.0 5.1 %collective-permute-done = bf16[7,64,512]{2,1,0:T(8,128)(2,1)S(1)} collective-permute-done((bf16[7,64,512]{2,1,0:T(8,128)(2,1)S(1)}, bf16[7,64,512]{2,1,0:T(8,128)(2,1)S(1)}, u32[]{:S(2)}, u32[]{:S(2)}) %collective-permute-start) | collective-permute-done | bytes 458784 | tf_op jit(solution)/shard_map/while/body/eval_jaxpr/ppermute | solution.py:33
  33.3 0.6 dynamic_slice.41
  34.5 0.3 fusion.29
  34.9 0.2 subtract_maximum_fusion.3
  35.1 0.3 fusion.30
  35.4 0.2 maximum_multiply_fusion.5
  35.6 0.7 %fusion.31 = f32[64,4,128]{2,0,1:T(8,128)S(1)} fusion(f32[512,4,128]{2,0,1:T(8,128)S(1)} %subtract_maximum_fusion.3, f32[7,512,128]{2,1,0:T(8,128)S(1)} %maximum_multiply_fusion.5, bf16[7,64,512]{2,1,0:T(8,128)(2,1)S(1)} %copy.14), kind=kOutput, calls=%fused_computation.5.clone.1 | convolution fusion | flops 238551040 | bytes 3473408 | tf_op jit(solution)/shard_map/while/body/eval_jaxpr/kts,kswo->two/dot_general | solution.py:89
  36.3 0.6 dynamic_slice.42
  38.8 0.4 add.173
  39.2 5.0 %collective-permute-done = bf16[7,64,512]{2,1,0:T(8,128)(2,1)S(1)} collective-permute-done((bf16[7,64,512]{2,1,0:T(8,128)(2,1)S(1)}, bf16[7,64,512]{2,1,0:T(8,128)(2,1)S(1)}, u32[]{:S(2)}, u32[]{:S(2)}) %collective-permute-start) | collective-permute-done | bytes 458784 | tf_op jit(solution)/shard_map/while/body/eval_jaxpr/ppermute | solution.py:33
  44.3 0.6 dynamic_slice.41
  45.6 0.3 fusion.29
  46.0 0.2 subtract_maximum_fusion.3
  46.2 0.3 fusion.30
  46.4 0.2 maximum_multiply_fusion.5
  46.6 0.7 %fusion.31 = f32[64,4,128]{2,0,1:T(8,128)S(1)} fusion(f32[512,4,128]{2,0,1:T(8,128)S(1)} %subtract_maximum_fusion.3, f32[7,512,128]{2,1,0:T(8,128)S(1)} %maximum_multiply_fusion.5, bf16[7,64,512]{2,1,0:T(8,128)(2,1)S(1)} %copy.14), kind=kOutput, calls=%fused_computation.5.clone.1 | convolution fusion | flops 238551040 | bytes 3473408 | tf_op jit(solution)/shard_map/while/body/eval_jaxpr/kts,kswo->two/dot_general | solution.py:89
  47.4 0.6 dynamic_slice.42
  49.9 0.3 add.173
  50.2 4.1 %collective-permute-done = bf16[7,64,512]{2,1,0:T(8,128)(2,1)S(1)} collective-permute-done((bf16[7,64,512]{2,1,0:T(8,128)(2,1)S(1)}, bf16[7,64,512]{2,1,0:T(8,128)(2,1)S(1)}, u32[]{:S(2)}, u32[]{:S(2)}) %collective-permute-start) | collective-permute-done | bytes 458784 | tf_op jit(solution)/shard_map/while/body/eval_jaxpr/ppermute | solution.py:33
  54.3 2.0 %fusion.11 = f32[64,4,128]{2,0,1:T(8,128)S(1)} fusion(f32[512,4,128]{2,0,1:T(8,128)} %subtract_maximum_fusion.1, f32[7,512,128]{2,1,0:T(8,128)S(1)} %maximum_multiply_fusion.1, bf16[7,64,512]{2,1,0:T(8,128)(2,1)S(1)} %get-tuple-element.111), kind=kOutput, calls=%fused_computation.29 | convolution fusion | flops 238551040 | bytes 3473408 | tf_op jit(solution)/shard_map/kts,kswo->two/dot_general | solution.py:89
  56.3 0.4 add.142
  56.7 6.9 %collective-permute-start.3 = (f32[64,128]{1,0:T(8,128)S(1)}, f32[64,128]{1,0:T(8,128)S(1)}, u32[]{:S(2)}, u32[]{:S(2)}) collective-permute-start(f32[64,128]{1,0:T(8,128)S(1)} %slice.102), channel_id=1, source_target_pairs={{0,1},{1,2},{2,3},{3,4},{4,5},{5,6},{6,7},{8,9},{9,10},{10,11},{11... | collective-permute-start | bytes 98312 | tf_op jit(solution)/shard_map/ppermute | solution.py:39
  63.6 1.0 %collective-permute-done.3 = f32[64,128]{1,0:T(8,128)S(1)} collective-permute-done((f32[64,128]{1,0:T(8,128)S(1)}, f32[64,128]{1,0:T(8,128)S(1)}, u32[]{:S(2)}, u32[]{:S(2)}) %collective-permute-start.3) | collective-permute-done | bytes 32800 | tf_op jit(solution)/shard_map/ppermute | solution.py:39
  64.6 0.6 slice_add_fusion
  (43 shorter events, 1.1 us)
Async XLA Ops:
  0.9 19.6 %collective-permute-start.2 = (f32[5,1,512]{2,1,0:T(1,128)S(1)}, f32[5,1,512]{2,1,0:T(1,128)S(1)}, u32[]{:S(2)}, u32[]{:S(2)}) collective-permute-start(f32[5,1,512]{2,1,0:T(1,128)S(1)} %get-tuple-element.143), channel_id=1, source_target_pairs={{1,0},{2,1},{3,2},{4,3},{5,4},{6,5},{7,6},{9,8},{10,9},{11,10},{12... | collective-permute-start | bytes 30728 | tf_op jit(solution)/shard_map/ppermute | solution.py:25
  2.9 17.7 %collective-permute-start.1 = (f32[5,1,512]{2,1,0:T(1,128)S(1)}, f32[5,1,512]{2,1,0:T(1,128)S(1)}, u32[]{:S(2)}, u32[]{:S(2)}) collective-permute-start(f32[5,1,512]{2,1,0:T(1,128)S(1)} %get-tuple-element.142), channel_id=1, source_target_pairs={{0,1},{1,2},{2,3},{3,4},{4,5},{5,6},{6,7},{8,9},{9,10},{10,11},{11... | collective-permute-start | bytes 30728 | tf_op jit(solution)/shard_map/ppermute | solution.py:22
  17.5 0.7 %copy-start.2 = (s32[4,4]{1,0:T(4,128)S(1)}, s32[4,4]{1,0:T(4,128)}, u32[]{:S(2)}) copy-start(s32[4,4]{1,0:T(4,128)} %param.11) | copy-start | bytes 196
  17.5 3.1 %copy-start = (f32[5,64,512]{2,1,0:T(8,128)S(1)}, f32[5,64,512]{2,1,0:T(8,128)}, u32[]{:S(2)}) copy-start(f32[5,64,512]{2,1,0:T(8,128)} %param.7) | copy-start | bytes 1966084
  18.1 2.7 %copy-start.1 = (f32[3,512]{1,0:T(4,128)S(1)}, f32[3,512]{1,0:T(4,128)}, u32[]{:S(2)}) copy-start(f32[3,512]{1,0:T(4,128)} %param.9) | copy-start | bytes 18436
  21.2 11.9 %collective-permute-start = (bf16[7,64,512]{2,1,0:T(8,128)(2,1)S(1)}, bf16[7,64,512]{2,1,0:T(8,128)(2,1)S(1)}, u32[]{:S(2)}, u32[]{:S(2)}) collective-permute-start(bf16[7,64,512]{2,1,0:T(8,128)(2,1)S(1)} %copy.14), channel_id=1, source_target_pairs={{24,0},{0,8},{8,16},{16,24},{25,1},{1,9},{9,17},{17,25},{26,2},{2,... | collective-permute-start | bytes 1376264 | tf_op jit(solution)/shard_map/while/body/eval_jaxpr/ppermute | solution.py:33
  33.2 11.0 %collective-permute-start = (bf16[7,64,512]{2,1,0:T(8,128)(2,1)S(1)}, bf16[7,64,512]{2,1,0:T(8,128)(2,1)S(1)}, u32[]{:S(2)}, u32[]{:S(2)}) collective-permute-start(bf16[7,64,512]{2,1,0:T(8,128)(2,1)S(1)} %copy.14), channel_id=1, source_target_pairs={{24,0},{0,8},{8,16},{16,24},{25,1},{1,9},{9,17},{17,25},{26,2},{2,... | collective-permute-start | bytes 1376264 | tf_op jit(solution)/shard_map/while/body/eval_jaxpr/ppermute | solution.py:33
  44.2 10.1 %collective-permute-start = (bf16[7,64,512]{2,1,0:T(8,128)(2,1)S(1)}, bf16[7,64,512]{2,1,0:T(8,128)(2,1)S(1)}, u32[]{:S(2)}, u32[]{:S(2)}) collective-permute-start(bf16[7,64,512]{2,1,0:T(8,128)(2,1)S(1)} %copy.14), channel_id=1, source_target_pairs={{24,0},{0,8},{8,16},{16,24},{25,1},{1,9},{9,17},{17,25},{26,2},{2,... | collective-permute-start | bytes 1376264 | tf_op jit(solution)/shard_map/while/body/eval_jaxpr/ppermute | solution.py:33
  56.7 7.9 %collective-permute-start.3 = (f32[64,128]{1,0:T(8,128)S(1)}, f32[64,128]{1,0:T(8,128)S(1)}, u32[]{:S(2)}, u32[]{:S(2)}) collective-permute-start(f32[64,128]{1,0:T(8,128)S(1)} %slice.102), channel_id=1, source_target_pairs={{0,1},{1,2},{2,3},{3,4},{4,5},{5,6},{6,7},{8,9},{9,10},{10,11},{11... | collective-permute-start | bytes 98312 | tf_op jit(solution)/shard_map/ppermute | solution.py:39
where the time goes:
time: 65.8 us; the launch traced here: 65.2 us
  waiting for transfers between devices  15.2 us (23%)
  starting transfers between devices  14.4 us (22%)
  other arithmetic  7.71 us (12%)
  loops' own time  7.7 us (12%)
  local copies, waits for them, and re-layouts  7.33 us (11%)
  blocking collectives  6.57 us (10%)
  matrix products  4.21 us (6%)
  between operations  2.08 us (3%)
    ppermute x3, waiting for transfers between devices, from_behind(): return lax.ppermute(block, axis, route)  14.2 us
    another operation x1, loops' own time, local(): lax.scan(turn, (initial, terms), jnp.arange(block_total - 1, dtype=jnp.in...  7.7 us
    ppermute x1, starting transfers between devices, passed_along(): return lax.ppermute(block, axis, route)  6.9 us
    all_gather x1, blocking collectives, local(): every_point = lax.all_gather(point_pos, 'obs', axis=1, tiled=True)  6.57 us
    ppermute x1, starting transfers between devices, extended(): lax.ppermute(lax.slice_in_dim(block, block.shape[dim] - width, None, axis...  4.55 us
    dot_general x4, matrix products, placed(): jnp.einsum('kts,kswo->two', shard_terms, weights, preferred_element_type=...  4.21 us
    dynamic_slice x4, local copies, waits for them, and re-layouts, add_block(): delays[block_index]  2.45 us
    ppermute x1, starting transfers between devices, extended(): lax.ppermute(lax.slice_in_dim(block, 0, width, axis=dim), axis, backward)  1.97 us
  transfers between devices with their start and end apart: 6, of which 4 were waited for; matrix products, arithmetic and copies ran while one was open for 22% of the time, Pallas kernels for 0%

commit v1 on v0

v1 whole, which is shorter than its diff:
```python
import functools
import math

import jax
import jax.numpy as jnp
from jax import lax
from jax.experimental import pallas as pl
from jax.experimental.pallas import tpu as pltpu
from jax.sharding import PartitionSpec as P

LAGS = 4
FOUR_PI = 4.0 * math.pi
NEAR_RANGE = 3.25
SOUND_STEP = 1.17
SPHERE_RADIUS = 5.0
MESH = pl.DeviceIdType.MESH
F32 = jnp.float32
BF16 = jnp.bfloat16
TAIL = 8
CHUNK = 64


def split3(x):
    high = x.astype(BF16).astype(F32)
    rest = x - high
    mid = rest.astype(BF16).astype(F32)
    low = (rest - mid).astype(BF16).astype(F32)
    return high, mid, low


def squares(x):
    return x[0:1] * x[0:1] + x[1:2] * x[1:2] + x[2:3] * x[2:3]


def point_factors(points):
    scaled = FOUR_PI * points
    high, mid, low = split3(scaled)
    s_high, s_mid, s_low = split3(squares(scaled))
    ones = jnp.ones((3, points.shape[1]), F32)
    pad = jnp.zeros((8, points.shape[1]), F32)
    rows = [high, high, mid, high, low, mid, s_high, s_mid, s_low, ones, pad]
    return jnp.concatenate(rows, axis=0)


def observer_factors(places):
    scaled = FOUR_PI * places
    high, mid, low = split3(-2.0 * scaled)
    s_high, s_mid, s_low = split3(squares(scaled))
    ones = jnp.ones((3, places.shape[1]), F32)
    pad = jnp.zeros((8, places.shape[1]), F32)
    rows = [high, mid, high, low, high, mid, ones, s_high, s_mid, s_low, pad]
    return jnp.concatenate(rows, axis=0)


def fluxes(flow, area):
    density = 1.0 + 0.2 * flow[0]
    velocity = [0.4 * flow[1 + i] for i in range(3)]
    normal = velocity[0] * area[0:1] + velocity[1] * area[1:2] + velocity[2] * area[2:3]
    mass = density * normal
    return [mass] + [flow[4] * area[i : i + 1] + density * velocity[i] * normal for i in range(3)]


def kernel(
    groups, blocks,
    flow_hbm, pos_hbm, area_hbm, angles_hbm, band_hbm, out_ref,
    flow, pos, area, angles, band, places, edge_out, edge_in, flux, steady_rate, mass_rate,
    w_mass, w_load, sent, landed,
    in_sem, place_send, place_recv, edge_send, edge_recv, part_send, part_recv,
):
    me = lax.axis_index("obs")
    now = lax.axis_index("tm")
    steps = flow.shape[1]
    points = flow.shape[2]
    has_before = now > 0
    has_after = now < blocks - 1

    barrier = pltpu.get_barrier_semaphore()

    def greet(group, block):
        pl.semaphore_signal(barrier, inc=1, device_id=(group, block), device_id_type=MESH)

    for i in range(1, groups):
        greet(lax.rem(me + i, groups), now)

    @pl.when(has_before)
    def _():
        for i in range(groups):
            greet(lax.rem(me + i, groups), now - 1)

    @pl.when(has_after)
    def _():
        for i in range(groups):
            greet(lax.rem(me + i, groups), now + 1)

    loads = [
        pltpu.make_async_copy(source, target, in_sem.at[i])
        for i, (source, target) in enumerate(
            [(angles_hbm, angles), (flow_hbm, flow), (area_hbm, area), (pos_hbm, pos), (band_hbm, band)]
        )
    ]
    for load in loads:
        load.start()

    loads[0].wait()
    azimuth = angles[0:1, :]
    elevation = angles[1:2, :]
    cos_e = jnp.cos(elevation)
    width = azimuth.shape[1]
    places[me] = jnp.concatenate(
        [
            SPHERE_RADIUS * (jnp.cos(azimuth) * cos_e),
            SPHERE_RADIUS * (jnp.sin(azimuth) * cos_e),
            SPHERE_RADIUS * jnp.sin(elevation),
            jnp.zeros((5, width), F32),
        ],
        axis=0,
    )

    loads[1].wait()
    loads[2].wait()
    area_rows = area[...]
    whole = fluxes(flow, area_rows)
    for k in range(4):
        flux[k] = whole[k]
    edge_pad = jnp.zeros((4, points), F32)
    edge_out[0] = jnp.concatenate([flux[k, 0:1, :] for k in range(4)] + [edge_pad], axis=0)
    edge_out[1] = jnp.concatenate(
        [flux[k, steps - 1 : steps, :] for k in range(4)] + [edge_pad], axis=0
    )

    neighbours = jnp.minimum(now, 1) + jnp.minimum(blocks - 1 - now, 1)
    pl.semaphore_wait(barrier, groups - 1 + groups * neighbours)

    def place_copy(i):
        return pltpu.make_async_remote_copy(
            src_ref=places.at[me], dst_ref=places.at[me],
            send_sem=place_send.at[i], recv_sem=place_recv.at[me],
            device_id=(lax.rem(me + i, groups), now), device_id_type=MESH,
        )

    def edge_copy(side, block):
        return pltpu.make_async_remote_copy(
            src_ref=edge_out.at[side], dst_ref=edge_in.at[side],
            send_sem=edge_send.at[side], recv_sem=edge_recv.at[side],
            device_id=(me, block), device_id_type=MESH,
        )

    for i in range(1, groups):
        place_copy(i).start()

    @pl.when(has_before)
    def _():
        edge_copy(0, now - 1).start()

    @pl.when(has_after)
    def _():
        edge_copy(1, now + 1).start()

    for j in range(2):
        for b in range(groups):
            landed[j, b, 0:steps, :] = jnp.zeros((steps, width), F32)
            landed[j, b, 2 * steps + TAIL :, :] = jnp.zeros((steps - TAIL, width), F32)

    loads[3].wait()
    loads[4].wait()
    spots = pos[...]
    factors = jnp.transpose(point_factors(spots)).astype(BF16)
    spot_rows = [spots[i : i + 1, :] for i in range(3)]

    def with_projection(parts):
        rounded = [part.astype(BF16) for part in parts]
        wide = [part.astype(F32) for part in rounded]
        along = wide[0] * spot_rows[0] + wide[1] * spot_rows[1] + wide[2] * spot_rows[2]
        return jnp.concatenate(rounded + [(-along).astype(BF16)], axis=0)

    steady_rate[:, points:] = with_projection([flux[1 + k] for k in range(3)])

    @pl.when(has_before)
    def _():
        edge_copy(1, now - 1).wait_recv()

    @pl.when(has_after)
    def _():
        edge_copy(0, now + 1).wait_recv()

    @pl.when(jnp.logical_not(has_before))
    def _():
        edge_in[1] = jnp.zeros((8, points), F32)

    @pl.when(jnp.logical_not(has_after))
    def _():
        edge_in[0] = jnp.zeros((8, points), F32)

    row = lax.broadcasted_iota(jnp.int32, (steps, points), 0)
    rates = []
    for k in range(4):
        mine = flux[k]
        later = jnp.where(row == steps - 1, edge_in[0, k : k + 1, :], pltpu.roll(mine, steps - 1, 0))
        earlier = jnp.where(row == 0, edge_in[1, k : k + 1, :], pltpu.roll(mine, 1, 0))
        rates.append(0.5 * (later - earlier))
    mass_rate[...] = rates[0].astype(BF16)
    steady_rate[:, :points] = with_projection(rates[1:])

    near = 1.0 / (SOUND_STEP * FOUR_PI)
    slope = NEAR_RANGE / SOUND_STEP

    def weigh(slot, group_places):
        squared = jnp.dot(
            factors, observer_factors(group_places).astype(BF16), preferred_element_type=F32
        )
        for start in range(0, points, CHUNK):
            rows = slice(start, start + CHUNK)
            load_rows = slice(points + start, points + start + CHUNK)
            r = lax.rsqrt(squared[rows])
            u = near - slope * r
            z = u - r
            y = z - r
            tents = [
                jnp.maximum(0.0, -z),
                jnp.maximum(0.0, jnp.minimum(u, -y)),
                jnp.maximum(0.0, jnp.minimum(z, r - y)),
                jnp.maximum(0.0, y),
            ]
            by_rate = r * (FOUR_PI / SOUND_STEP)
            by_load = r * r * (FOUR_PI * FOUR_PI)
            for j in range(LAGS):
                columns = slice(j * width, (j + 1) * width)
                w_mass[slot, rows, columns] = tents[j].astype(BF16)
                w_load[slot, rows, columns] = (tents[j] * by_rate).astype(BF16)
                w_load[slot, load_rows, columns] = (tents[j] * by_load).astype(BF16)

    def part_copy(i, group, later):
        return pltpu.make_async_remote_copy(
            src_ref=sent.at[group], dst_ref=landed.at[later, me, pl.ds(steps, steps + TAIL), :],
            send_sem=part_send.at[later, i], recv_sem=part_recv.at[later, me],
            device_id=(group, now + later), device_id_type=MESH,
        )

    for i in range(groups):
        group = lax.rem(me + i, groups)
        if i > 0:
            pltpu.make_async_remote_copy(
                src_ref=places.at[group], dst_ref=places.at[group],
                send_sem=place_send.at[i], recv_sem=place_recv.at[group],
                device_id=(group, now), device_id_type=MESH,
            ).wait_recv()
        slot = i % 2
        group_places = places[group][0:3]
        weigh(slot, group_places)
        by_mass = jnp.dot(mass_rate[...], w_mass[slot], preferred_element_type=F32)
        by_load = jnp.dot(steady_rate[...], w_load[slot], preferred_element_type=F32)
        total = jnp.zeros((steps + TAIL, width), F32)
        for j in range(LAGS):
            columns = slice(j * width, (j + 1) * width)
            piece = by_mass[:, columns] + by_load[3 * steps :, columns]
            for k in range(3):
                piece = piece + by_load[k * steps : (k + 1) * steps, columns] * group_places[k : k + 1]
            piece = jnp.concatenate([piece, jnp.zeros((TAIL, width), F32)], axis=0)
            total = total + (pltpu.roll(piece, j, 0) if j else piece)
        sent[group] = total
        if i > 0:
            part_copy(i, group, 0).start()
        else:
            landed[0, me, steps : 2 * steps + TAIL, :] = total

        @pl.when(has_after)
        def _():
            part_copy(i, group, 1).start()

    def arrived(later, block):
        return pltpu.make_async_remote_copy(
            src_ref=sent.at[0], dst_ref=landed.at[later, block, pl.ds(steps, steps + TAIL), :],
            send_sem=part_send.at[later, 0], recv_sem=part_recv.at[later, block],
            device_id=(lax.rem(me + 1, groups), now), device_id_type=MESH,
        )

    for i in range(1, groups):
        arrived(0, lax.rem(me + i, groups)).wait_recv()

    @pl.when(has_before)
    def _():
        for b in range(groups):
            arrived(1, b).wait_recv()

    @pl.when(jnp.logical_not(has_before))
    def _():
        for b in range(groups):
            landed[1, b, steps : 2 * steps + TAIL, :] = jnp.zeros((steps + TAIL, width), F32)

    result = jnp.zeros((steps, width), F32)
    for b in range(groups):
        offset = band[me, b]
        result = result + landed[0, b, pl.ds(steps - offset, steps), :]
        result = result + landed[1, b, pl.ds(2 * steps - offset, steps), :]
    out_ref[...] = result

    for i in range(1, groups):
        place_copy(i).wait_send()
        part_copy(i, lax.rem(me + i, groups), 0).wait_send()

    @pl.when(has_before)
    def _():
        edge_copy(0, now - 1).wait_send()

    @pl.when(has_after)
    def _():
        edge_copy(1, now + 1).wait_send()
        for i in range(groups):
            part_copy(i, lax.rem(me + i, groups), 1).wait_send()


def solution(mesh):
    groups = mesh.shape["obs"]
    blocks = mesh.shape["tm"]

    def local(flow, point_pos, area_vec, observer_angles, band_offset):
        steps, points = flow.shape[1:]
        width = observer_angles.shape[1]
        any_spec = pl.BlockSpec(memory_space=pl.ANY)
        dma = pltpu.SemaphoreType.DMA
        return pl.pallas_call(
            functools.partial(kernel, groups, blocks),
            out_shape=jax.ShapeDtypeStruct((steps, width), F32),
            in_specs=[any_spec] * 5,
            out_specs=pl.BlockSpec(memory_space=pltpu.VMEM),
            scratch_shapes=[
                pltpu.VMEM(flow.shape, F32),
                pltpu.VMEM(point_pos.shape, F32),
                pltpu.VMEM(area_vec.shape, F32),
                pltpu.VMEM(observer_angles.shape, F32),
                pltpu.SMEM(band_offset.shape, jnp.int32),
                pltpu.VMEM((groups, 8, width), F32),
                pltpu.VMEM((2, 8, points), F32),
                pltpu.VMEM((2, 8, points), F32),
                pltpu.VMEM((4, steps, points), F32),
                pltpu.VMEM((4 * steps, 2 * points), BF16),
                pltpu.VMEM((steps, points), BF16),
                pltpu.VMEM((2, points, LAGS * width), BF16),
                pltpu.VMEM((2, 2 * points, LAGS * width), BF16),
                pltpu.VMEM((groups, steps + TAIL, width), F32),
                pltpu.VMEM((2, groups, 3 * steps, width), F32),
                dma((5,)),
                dma((groups,)),
                dma((groups,)),
                dma((2,)),
                dma((2,)),
                dma((2, groups)),
                dma((2, groups)),
            ],
            compiler_params=pltpu.CompilerParams(
                collective_id=0, has_side_effects=True, vmem_limit_bytes=40 * 1024 * 1024
            ),
        )(flow, point_pos, area_vec, observer_angles, band_offset)

    in_specs = (P(None, "tm", "obs"), P(None, "obs"), P(None, "obs"), P(None, "obs"), P())
    return jax.shard_map(
        local, mesh=mesh, in_specs=in_specs, out_specs=P("tm", "obs"), check_vma=False
    )
```

time: 65.8 us -> 17.5 us (0.27)
  the two profiles are of different devices: /device:TPU:1 before, /device:TPU:0 now
where the time goes in v1:
time: 17.5 us; the launch traced here: 17.2 us
  Pallas kernels  12.7 us (73%)
  local copies, waits for them, and re-layouts  4.46 us (25%)
    pallas_call x1, Pallas kernels, local(): pl.pallas_call(functools.partial(kernel, groups, blocks), out_shape=jax.S...  12.7 us
    unnamed x11, local copies, waits for them, and re-layouts  4.46 us

profile of v1, /device:TPU:0, one launch (start us, length us, event | category | flops | bytes accessed | tf_op | source)
XLA Modules:
  0.0 17.2 jit_solution(6410992791504448504)
XLA Ops:
  0.0 0.0 copy-start
  0.0 1.1 %copy-done = f32[5,64,512]{2,1,0:T(8,128)S(1)} copy-done((f32[5,64,512]{2,1,0:T(8,128)S(1)}, f32[5,64,512]{2,1,0:T(8,128)}, u32[]{:S(2)}) %copy-start) | copy-done | bytes 655384
  1.1 0.0 copy-start.1
  1.1 0.7 %copy-done.1 = f32[3,512]{1,0:T(4,128)S(1)} copy-done((f32[3,512]{1,0:T(4,128)S(1)}, f32[3,512]{1,0:T(4,128)}, u32[]{:S(2)}) %copy-start.1) | copy-done | bytes 6168
  1.8 0.0 copy-start.2
  1.8 0.7 %copy-done.2 = f32[3,512]{1,0:T(4,128)S(1)} copy-done((f32[3,512]{1,0:T(4,128)S(1)}, f32[3,512]{1,0:T(4,128)}, u32[]{:S(2)}) %copy-start.2) | copy-done | bytes 6168
  2.5 0.0 copy-start.3
  2.5 0.7 %copy-done.3 = s32[4,4]{1,0:T(4,128)S(1)} copy-done((s32[4,4]{1,0:T(4,128)S(1)}, s32[4,4]{1,0:T(4,128)}, u32[]{:S(2)}) %copy-start.3) | copy-done | bytes 88
  3.2 0.0 copy-start.4
  3.2 0.7 %copy-done.4 = f32[2,128]{1,0:T(2,128)S(1)} copy-done((f32[2,128]{1,0:T(2,128)S(1)}, f32[2,128]{1,0:T(2,128)}, u32[]{:S(2)}) %copy-start.4) | copy-done | bytes 1048
  3.8 12.7 %shard_map.55 = f32[64,128]{1,0:T(8,128)S(1)} custom-call(f32[5,64,512]{2,1,0:T(8,128)S(1)} %copy-done, f32[3,512]{1,0:T(4,128)S(1)} %copy-done.1, f32[3,512]{1,0:T(4,128)S(1)} %copy-done.2, f32[2,128]{1,0:T(2,128)S(1)} %copy-done.4, s32[4,4]{1,0:T(4,128)S(1)} %copy-done.3), custom_call_target="tpu_custom_call" | custom-call | tf_op jit(solution)/shard_map/pallas_call | solution.py:321
  16.6 0.6 %copy.7 = f32[64,128]{1,0:T(8,128)} copy(f32[64,128]{1,0:T(8,128)S(1)} %shard_map.55) | data formatting | bytes 65536
Async XLA Ops:
  0.0 1.1 %copy-start = (f32[5,64,512]{2,1,0:T(8,128)S(1)}, f32[5,64,512]{2,1,0:T(8,128)}, u32[]{:S(2)}) copy-start(f32[5,64,512]{2,1,0:T(8,128)} %flow_hbm.1) | copy-start | bytes 1966084
  1.1 0.7 %copy-start.1 = (f32[3,512]{1,0:T(4,128)S(1)}, f32[3,512]{1,0:T(4,128)}, u32[]{:S(2)}) copy-start(f32[3,512]{1,0:T(4,128)} %pos_hbm.1) | copy-start | bytes 18436
  1.8 0.7 %copy-start.2 = (f32[3,512]{1,0:T(4,128)S(1)}, f32[3,512]{1,0:T(4,128)}, u32[]{:S(2)}) copy-start(f32[3,512]{1,0:T(4,128)} %area_hbm.1) | copy-start | bytes 18436
  2.5 0.7 %copy-start.3 = (s32[4,4]{1,0:T(4,128)S(1)}, s32[4,4]{1,0:T(4,128)}, u32[]{:S(2)}) copy-start(s32[4,4]{1,0:T(4,128)} %band_hbm.1) | copy-start | bytes 196
  3.2 0.7 %copy-start.4 = (f32[2,128]{1,0:T(2,128)S(1)}, f32[2,128]{1,0:T(2,128)}, u32[]{:S(2)}) copy-start(f32[2,128]{1,0:T(2,128)} %angles_hbm.1) | copy-start | bytes 3076

commit v2 on v1

--- a/solution.py
+++ b/solution.py
@@ -71,6 +71,15 @@
     now = lax.axis_index("tm")
     steps = flow.shape[1]
     points = flow.shape[2]
+    side = math.isqrt(groups)
+    if side * side != groups:
+        side = groups
+    high, low = me // side, lax.rem(me, side)
+    shifts = [(i, j) for i in range(groups // side) for j in range(side)]
+    shifts.sort(key=lambda pair: (pair != (0, 0), -min(pair), -sum(pair)))
+    order = [
+        lax.rem(high + i, groups // side) * side + lax.rem(low + j, side) for i, j in shifts
+    ]
     has_before = now > 0
     has_after = now < blocks - 1
 
@@ -80,17 +89,17 @@
         pl.semaphore_signal(barrier, inc=1, device_id=(group, block), device_id_type=MESH)
 
     for i in range(1, groups):
-        greet(lax.rem(me + i, groups), now)
+        greet(order[i], now)
 
     @pl.when(has_before)
     def _():
         for i in range(groups):
-            greet(lax.rem(me + i, groups), now - 1)
+            greet(order[i], now - 1)
 
     @pl.when(has_after)
     def _():
         for i in range(groups):
-            greet(lax.rem(me + i, groups), now + 1)
+            greet(order[i], now + 1)
 
     loads = [
         pltpu.make_async_copy(source, target, in_sem.at[i])
@@ -135,7 +144,7 @@
         return pltpu.make_async_remote_copy(
             src_ref=places.at[me], dst_ref=places.at[me],
             send_sem=place_send.at[i], recv_sem=place_recv.at[me],
-            device_id=(lax.rem(me + i, groups), now), device_id_type=MESH,
+            device_id=(order[i], now), device_id_type=MESH,
         )
 
     def edge_copy(side, block):
@@ -174,32 +183,6 @@
         return jnp.concatenate(rounded + [(-along).astype(BF16)], axis=0)
 
     steady_rate[:, points:] = with_projection([flux[1 + k] for k in range(3)])
-
-    @pl.when(has_before)
-    def _():
-        edge_copy(1, now - 1).wait_recv()
-
-    @pl.when(has_after)
-    def _():
-        edge_copy(0, now + 1).wait_recv()
-
-    @pl.when(jnp.logical_not(has_before))
-    def _():
-        edge_in[1] = jnp.zeros((8, points), F32)
-
-    @pl.when(jnp.logical_not(has_after))
-    def _():
-        edge_in[0] = jnp.zeros((8, points), F32)
-
-    row = lax.broadcasted_iota(jnp.int32, (steps, points), 0)
-    rates = []
-    for k in range(4):
-        mine = flux[k]
-        later = jnp.where(row == steps - 1, edge_in[0, k : k + 1, :], pltpu.roll(mine, steps - 1, 0))
-        earlier = jnp.where(row == 0, edge_in[1, k : k + 1, :], pltpu.roll(mine, 1, 0))
-        rates.append(0.5 * (later - earlier))
-    mass_rate[...] = rates[0].astype(BF16)
-    steady_rate[:, :points] = with_projection(rates[1:])
 
     near = 1.0 / (SOUND_STEP * FOUR_PI)
     slope = NEAR_RANGE / SOUND_STEP
@@ -236,17 +219,48 @@
             device_id=(group, now + later), device_id_type=MESH,
         )
 
+    def await_places(i):
+        pltpu.make_async_remote_copy(
+            src_ref=places.at[order[i]], dst_ref=places.at[order[i]],
+            send_sem=place_send.at[i], recv_sem=place_recv.at[order[i]],
+            device_id=(order[i], now), device_id_type=MESH,
+        ).wait_recv()
+
+    weigh(0, places[me][0:3])
+
+    @pl.when(has_before)
+    def _():
+        edge_copy(1, now - 1).wait_recv()
+
+    @pl.when(has_after)
+    def _():
+        edge_copy(0, now + 1).wait_recv()
+
+    @pl.when(jnp.logical_not(has_before))
+    def _():
+        edge_in[1] = jnp.zeros((8, points), F32)
+
+    @pl.when(jnp.logical_not(has_after))
+    def _():
+        edge_in[0] = jnp.zeros((8, points), F32)
+
+    row = lax.broadcasted_iota(jnp.int32, (steps, points), 0)
+    rates = []
+    for k in range(4):
+        mine = flux[k]
+        later = jnp.where(row == steps - 1, edge_in[0, k : k + 1, :], pltpu.roll(mine, steps - 1, 0))
+        earlier = jnp.where(row == 0, edge_in[1, k : k + 1, :], pltpu.roll(mine, 1, 0))
+        rates.append(0.5 * (later - earlier))
+    mass_rate[...] = rates[0].astype(BF16)
+    steady_rate[:, :points] = with_projection(rates[1:])
+
     for i in range(groups):
-        group = lax.rem(me + i, groups)
-        if i > 0:
-            pltpu.make_async_remote_copy(
-                src_ref=places.at[group], dst_ref=places.at[group],
-                send_sem=place_send.at[i], recv_sem=place_recv.at[group],
-                device_id=(group, now), device_id_type=MESH,
-            ).wait_recv()
+        group = order[i]
         slot = i % 2
+        if i + 1 < groups:
+            await_places(i + 1)
+            weigh(1 - slot, places[order[i + 1]][0:3])
         group_places = places[group][0:3]
-        weigh(slot, group_places)
         by_mass = jnp.dot(mass_rate[...], w_mass[slot], preferred_element_type=F32)
         by_load = jnp.dot(steady_rate[...], w_load[slot], preferred_element_type=F32)
         total = jnp.zeros((steps + TAIL, width), F32)
@@ -271,11 +285,11 @@
         return pltpu.make_async_remote_copy(
             src_ref=sent.at[0], dst_ref=landed.at[later, block, pl.ds(steps, steps + TAIL), :],
             send_sem=part_send.at[later, 0], recv_sem=part_recv.at[later, block],
-            device_id=(lax.rem(me + 1, groups), now), device_id_type=MESH,
+            device_id=(order[1], now), device_id_type=MESH,
         )
 
     for i in range(1, groups):
-        arrived(0, lax.rem(me + i, groups)).wait_recv()
+        arrived(0, order[i]).wait_recv()
 
     @pl.when(has_before)
     def _():
@@ -296,7 +310,7 @@
 
     for i in range(1, groups):
         place_copy(i).wait_send()
-        part_copy(i, lax.rem(me + i, groups), 0).wait_send()
+        part_copy(i, order[i], 0).wait_send()
 
     @pl.when(has_before)
     def _():
@@ -306,7 +320,7 @@
     def _():
         edge_copy(1, now + 1).wait_send()
         for i in range(groups):
-            part_copy(i, lax.rem(me + i, groups), 1).wait_send()
+            part_copy(i, order[i], 1).wait_send()
 
 
 def solution(mesh):
@@ -348,7 +362,7 @@
                 dma((2, groups)),
             ],
             compiler_params=pltpu.CompilerParams(
-                collective_id=0, has_side_effects=True, vmem_limit_bytes=40 * 1024 * 1024
+                collective_id=0, has_side_effects=True, vmem_limit_bytes=64 * 1024 * 1024
             ),
         )(flow, point_pos, area_vec, observer_angles, band_offset)
 

time: 17.5 us -> 15.6 us (0.89)
  local copies, waits for them, and re-layouts: 4.46 us -> 1.38 us
  Pallas kernels: 12.7 us -> 14.1 us
    unnamed x11 -> x1, local copies, waits for them, and re-layouts: 4.46 us -> 1.38 us
    pallas_call x1, Pallas kernels: 12.7 us -> 14.1 us  [local(): pl.pallas_call(functools.partial(kernel, groups, blocks), out_shape=jax.S...]
where the time goes in v2:
time: 15.6 us; the launch traced here: 15.4 us
  Pallas kernels  14.1 us (90%)
  local copies, waits for them, and re-layouts  1.38 us (9%)
    pallas_call x1, Pallas kernels, local(): pl.pallas_call(functools.partial(kernel, groups, blocks), out_shape=jax.S...  14.1 us
    unnamed x1, local copies, waits for them, and re-layouts  1.38 us

profile of v2, /device:TPU:0, one launch (start us, length us, event | category | flops | bytes accessed | tf_op | source)
XLA Modules:
  0.0 15.4 jit_solution(5890201749879580648)
XLA Ops:
  0.0 14.1 %shard_map.55 = f32[64,128]{1,0:T(8,128)} custom-call(f32[5,64,512]{2,1,0:T(8,128)} %flow_hbm.1, f32[3,512]{1,0:T(4,128)} %pos_hbm.1, f32[3,512]{1,0:T(4,128)} %area_hbm.1, f32[2,128]{1,0:T(2,128)} %angles_hbm.1, s32[4,4]{1,0:T(4,128)} %band_hbm.1), custom_call_target="tpu_custom_call" | custom-call | tf_op jit(solution)/shard_map/pallas_call | solution.py:335
  14.1 1.4 %copy.7 = f32[64,128]{1,0:T(8,128)} copy(f32[64,128]{1,0:T(8,128)} %shard_map.55) | data formatting | bytes 65536

commit v3 on v2

--- a/solution.py
+++ b/solution.py
@@ -362,9 +362,14 @@
                 dma((2, groups)),
             ],
             compiler_params=pltpu.CompilerParams(
-                collective_id=0, has_side_effects=True, vmem_limit_bytes=64 * 1024 * 1024
+                collective_id=0, has_side_effects=True, vmem_limit_bytes=40 * 1024 * 1024
             ),
-        )(flow, point_pos, area_vec, observer_angles, band_offset)
+        )(
+            *[
+                pltpu.with_memory_space_constraint(x, pltpu.HBM)
+                for x in (flow, point_pos, area_vec, observer_angles, band_offset)
+            ]
+        )
 
     in_specs = (P(None, "tm", "obs"), P(None, "obs"), P(None, "obs"), P(None, "obs"), P())
     return jax.shard_map(

time: 15.6 us -> 14.2 us (0.910)
  local copies, waits for them, and re-layouts: 1.38 us -> 0.62 us
  Pallas kernels: 14.1 us -> 13.4 us
    unnamed x1, local copies, waits for them, and re-layouts: 1.38 us -> 0.62 us
    pallas_call x1, Pallas kernels: 14.1 us -> 13.4 us  [local(): pl.pallas_call(functools.partial(kernel, groups, blocks), out_shape=jax.S...]
where the time goes in v3:
time: 14.2 us; the launch traced here: 14.1 us
  Pallas kernels  13.4 us (94%)
  local copies, waits for them, and re-layouts  0.62 us (4%)
    pallas_call x1, Pallas kernels, local(): pl.pallas_call(functools.partial(kernel, groups, blocks), out_shape=jax.S...  13.4 us
    unnamed x1, local copies, waits for them, and re-layouts  0.62 us

profile of v3, /device:TPU:0, one launch (start us, length us, event | category | flops | bytes accessed | tf_op | source)
XLA Modules:
  0.0 14.1 jit_solution(17868222897538892327)
XLA Ops:
  0.0 13.4 %shard_map.55 = f32[64,128]{1,0:T(8,128)S(1)} custom-call(f32[5,64,512]{2,1,0:T(8,128)} %flow_hbm.1, f32[3,512]{1,0:T(4,128)} %pos_hbm.1, f32[3,512]{1,0:T(4,128)} %area_hbm.1, f32[2,128]{1,0:T(2,128)} %angles_hbm.1, s32[4,4]{1,0:T(4,128)} %band_hbm.1), custom_call_target="tpu_custom_call" | custom-call | tf_op jit(solution)/shard_map/pallas_call | solution.py:335
  13.5 0.6 %copy.7 = f32[64,128]{1,0:T(8,128)} copy(f32[64,128]{1,0:T(8,128)S(1)} %shard_map.55) | data formatting | bytes 65536

commit v4 on v3

--- a/solution.py
+++ b/solution.py
@@ -64,9 +64,11 @@
     groups, blocks,
     flow_hbm, pos_hbm, area_hbm, angles_hbm, band_hbm, out_ref,
     flow, pos, area, angles, band, places, edge_out, edge_in, flux, steady_rate, mass_rate,
-    w_mass, w_load, sent, landed,
+    w_mass_low, w_mass_high, w_load_low, w_load_high, factors, inverse, sent, landed,
     in_sem, place_send, place_recv, edge_send, edge_recv, part_send, part_recv,
 ):
+    w_mass = (w_mass_low, w_mass_high)
+    w_load = (w_load_low, w_load_high)
     me = lax.axis_index("obs")
     now = lax.axis_index("tm")
     steps = flow.shape[1]
@@ -75,11 +77,12 @@
     if side * side != groups:
         side = groups
     high, low = me // side, lax.rem(me, side)
-    shifts = [(i, j) for i in range(groups // side) for j in range(side)]
-    shifts.sort(key=lambda pair: (pair != (0, 0), -min(pair), -sum(pair)))
-    order = [
-        lax.rem(high + i, groups // side) * side + lax.rem(low + j, side) for i, j in shifts
-    ]
+
+    def order(i):
+        shift = lax.rem(groups - i, groups)
+        row_index = lax.rem(high + shift // side, groups // side)
+        return row_index * side + lax.rem(low + lax.rem(shift, side), side)
+
     has_before = now > 0
     has_after = now < blocks - 1
 
@@ -89,17 +92,17 @@
         pl.semaphore_signal(barrier, inc=1, device_id=(group, block), device_id_type=MESH)
 
     for i in range(1, groups):
-        greet(order[i], now)
+        greet(order(i), now)
 
     @pl.when(has_before)
     def _():
         for i in range(groups):
-            greet(order[i], now - 1)
+            greet(order(i), now - 1)
 
     @pl.when(has_after)
     def _():
         for i in range(groups):
-            greet(order[i], now + 1)
+            greet(order(i), now + 1)
 
     loads = [
         pltpu.make_async_copy(source, target, in_sem.at[i])
@@ -144,7 +147,7 @@
         return pltpu.make_async_remote_copy(
             src_ref=places.at[me], dst_ref=places.at[me],
             send_sem=place_send.at[i], recv_sem=place_recv.at[me],
-            device_id=(order[i], now), device_id_type=MESH,
+            device_id=(order(i), now), device_id_type=MESH,
         )
 
     def edge_copy(side, block):
@@ -173,7 +176,7 @@
     loads[3].wait()
     loads[4].wait()
     spots = pos[...]
-    factors = jnp.transpose(point_factors(spots)).astype(BF16)
+    factors[...] = jnp.transpose(point_factors(spots)).astype(BF16)
     spot_rows = [spots[i : i + 1, :] for i in range(3)]
 
     def with_projection(parts):
@@ -187,30 +190,36 @@
     near = 1.0 / (SOUND_STEP * FOUR_PI)
     slope = NEAR_RANGE / SOUND_STEP
 
-    def weigh(slot, group_places):
-        squared = jnp.dot(
-            factors, observer_factors(group_places).astype(BF16), preferred_element_type=F32
-        )
+    def weigh(pair, squared):
         for start in range(0, points, CHUNK):
             rows = slice(start, start + CHUNK)
             load_rows = slice(points + start, points + start + CHUNK)
-            r = lax.rsqrt(squared[rows])
+            if pair == 0:
+                r = lax.rsqrt(squared[rows])
+                inverse[rows, :] = r
+            else:
+                r = inverse[rows, :]
             u = near - slope * r
             z = u - r
             y = z - r
-            tents = [
-                jnp.maximum(0.0, -z),
-                jnp.maximum(0.0, jnp.minimum(u, -y)),
-                jnp.maximum(0.0, jnp.minimum(z, r - y)),
-                jnp.maximum(0.0, y),
-            ]
+            if pair == 0:
+                tents = [jnp.maximum(0.0, -z), jnp.maximum(0.0, jnp.minimum(u, -y))]
+            else:
+                tents = [jnp.maximum(0.0, jnp.minimum(z, r - y)), jnp.maximum(0.0, y)]
             by_rate = r * (FOUR_PI / SOUND_STEP)
             by_load = r * r * (FOUR_PI * FOUR_PI)
-            for j in range(LAGS):
+            for j in range(2):
                 columns = slice(j * width, (j + 1) * width)
-                w_mass[slot, rows, columns] = tents[j].astype(BF16)
-                w_load[slot, rows, columns] = (tents[j] * by_rate).astype(BF16)
-                w_load[slot, load_rows, columns] = (tents[j] * by_load).astype(BF16)
+                w_mass[pair][rows, columns] = tents[j].astype(BF16)
+                w_load[pair][rows, columns] = (tents[j] * by_rate).astype(BF16)
+                w_load[pair][load_rows, columns] = (tents[j] * by_load).astype(BF16)
+
+    def ranges(group):
+        return jnp.dot(
+            factors[...],
+            observer_factors(places[group][0:3]).astype(BF16),
+            preferred_element_type=F32,
+        )
 
     def part_copy(i, group, later):
         return pltpu.make_async_remote_copy(
@@ -221,12 +230,12 @@
 
     def await_places(i):
         pltpu.make_async_remote_copy(
-            src_ref=places.at[order[i]], dst_ref=places.at[order[i]],
-            send_sem=place_send.at[i], recv_sem=place_recv.at[order[i]],
-            device_id=(order[i], now), device_id_type=MESH,
+            src_ref=places.at[order(i)], dst_ref=places.at[order(i)],
+            send_sem=place_send.at[i], recv_sem=place_recv.at[order(i)],
+            device_id=(order(i), now), device_id_type=MESH,
         ).wait_recv()
 
-    weigh(0, places[me][0:3])
+    weigh(0, ranges(me))
 
     @pl.when(has_before)
     def _():
@@ -254,42 +263,59 @@
     mass_rate[...] = rates[0].astype(BF16)
     steady_rate[:, :points] = with_projection(rates[1:])
 
-    for i in range(groups):
-        group = order[i]
-        slot = i % 2
-        if i + 1 < groups:
-            await_places(i + 1)
-            weigh(1 - slot, places[order[i + 1]][0:3])
-        group_places = places[group][0:3]
-        by_mass = jnp.dot(mass_rate[...], w_mass[slot], preferred_element_type=F32)
-        by_load = jnp.dot(steady_rate[...], w_load[slot], preferred_element_type=F32)
+    def gathered(pair, group):
+        spot = places[group]
+        by_mass = jnp.dot(mass_rate[...], w_mass[pair][...], preferred_element_type=F32)
+        by_load = jnp.dot(steady_rate[...], w_load[pair][...], preferred_element_type=F32)
         total = jnp.zeros((steps + TAIL, width), F32)
-        for j in range(LAGS):
+        for j in range(2):
             columns = slice(j * width, (j + 1) * width)
             piece = by_mass[:, columns] + by_load[3 * steps :, columns]
             for k in range(3):
-                piece = piece + by_load[k * steps : (k + 1) * steps, columns] * group_places[k : k + 1]
+                piece = piece + by_load[k * steps : (k + 1) * steps, columns] * spot[k : k + 1]
             piece = jnp.concatenate([piece, jnp.zeros((TAIL, width), F32)], axis=0)
-            total = total + (pltpu.roll(piece, j, 0) if j else piece)
+            lag = 2 * pair + j
+            total = total + (pltpu.roll(piece, lag, 0) if lag else piece)
+        return total
+
+    def one_group(i, unused):
+        group = order(i)
+        sent[group] = gathered(0, group)
+        weigh(1, None)
+
+        @pl.when(i + 1 < groups)
+        def _():
+            await_places(i + 1)
+
+        total = sent[group] + gathered(1, group)
         sent[group] = total
-        if i > 0:
+        weigh(0, ranges(order(jnp.minimum(i + 1, groups - 1))))
+
+        @pl.when(i > 0)
+        def _():
             part_copy(i, group, 0).start()
-        else:
-            landed[0, me, steps : 2 * steps + TAIL, :] = total
+
+        @pl.when(i == 0)
+        def _():
+            landed[0, me, steps : 2 * steps + TAIL, :] = sent[me]
 
         @pl.when(has_after)
         def _():
             part_copy(i, group, 1).start()
+
+        return unused
+
+    lax.fori_loop(0, groups, one_group, 0)
 
     def arrived(later, block):
         return pltpu.make_async_remote_copy(
             src_ref=sent.at[0], dst_ref=landed.at[later, block, pl.ds(steps, steps + TAIL), :],
             send_sem=part_send.at[later, 0], recv_sem=part_recv.at[later, block],
-            device_id=(order[1], now), device_id_type=MESH,
+            device_id=(order(1), now), device_id_type=MESH,
         )
 
     for i in range(1, groups):
-        arrived(0, order[i]).wait_recv()
+        arrived(0, order(i)).wait_recv()
 
     @pl.when(has_before)
     def _():
@@ -310,7 +336,7 @@
 
     for i in range(1, groups):
         place_copy(i).wait_send()
-        part_copy(i, order[i], 0).wait_send()
+        part_copy(i, order(i), 0).wait_send()
 
     @pl.when(has_before)
     def _():
@@ -320,7 +346,7 @@
     def _():
         edge_copy(1, now + 1).wait_send()
         for i in range(groups):
-            part_copy(i, order[i], 1).wait_send()
+            part_copy(i, order(i), 1).wait_send()
 
 
 def solution(mesh):
@@ -349,8 +375,12 @@
                 pltpu.VMEM((4, steps, points), F32),
                 pltpu.VMEM((4 * steps, 2 * points), BF16),
                 pltpu.VMEM((steps, points), BF16),
-                pltpu.VMEM((2, points, LAGS * width), BF16),
-                pltpu.VMEM((2, 2 * points, LAGS * width), BF16),
+                pltpu.VMEM((points, LAGS // 2 * width), BF16),
+                pltpu.VMEM((points, LAGS // 2 * width), BF16),
+                pltpu.VMEM((2 * points, LAGS // 2 * width), BF16),
+                pltpu.VMEM((2 * points, LAGS // 2 * width), BF16),
+                pltpu.VMEM((points, 32), BF16),
+                pltpu.VMEM((points, width), F32),
                 pltpu.VMEM((groups, steps + TAIL, width), F32),
                 pltpu.VMEM((2, groups, 3 * steps, width), F32),
                 dma((5,)),

time: 14.2 us -> 14.9 us (1.049)
  Pallas kernels: 13.4 us -> 14.1 us
    pallas_call x1, Pallas kernels: 13.4 us -> 14.1 us  [local(): pl.pallas_call(functools.partial(kernel, groups, blocks), out_shape=jax.S...]
where the time goes in v4:
time: 14.9 us; the launch traced here: 14.8 us
  Pallas kernels  14.1 us (95%)
  local copies, waits for them, and re-layouts  0.62 us (4%)
    pallas_call x1, Pallas kernels, local(): pl.pallas_call(functools.partial(kernel, groups, blocks), out_shape=jax.S...  14.1 us
    unnamed x1, local copies, waits for them, and re-layouts  0.62 us

profile of v4, /device:TPU:0, one launch (start us, length us, event | category | flops | bytes accessed | tf_op | source)
XLA Modules:
  0.0 14.8 jit_solution(10368078569063567229)
XLA Ops:
  0.0 14.1 %shard_map.55 = f32[64,128]{1,0:T(8,128)S(1)} custom-call(f32[5,64,512]{2,1,0:T(8,128)} %flow_hbm.1, f32[3,512]{1,0:T(4,128)} %pos_hbm.1, f32[3,512]{1,0:T(4,128)} %area_hbm.1, f32[2,128]{1,0:T(2,128)} %angles_hbm.1, s32[4,4]{1,0:T(4,128)} %band_hbm.1), custom_call_target="tpu_custom_call" | custom-call | tf_op jit(solution)/shard_map/pallas_call | solution.py:361
  14.2 0.6 %copy.7 = f32[64,128]{1,0:T(8,128)} copy(f32[64,128]{1,0:T(8,128)S(1)} %shard_map.55) | data formatting | bytes 65536

commit v5 on v3

--- a/solution.py
+++ b/solution.py
@@ -50,6 +50,23 @@
     pad = jnp.zeros((8, places.shape[1]), F32)
     rows = [high, mid, high, low, high, mid, ones, s_high, s_mid, s_low, pad]
     return jnp.concatenate(rows, axis=0)
+
+
+def sine_cosine(x):
+    turns = jnp.floor(x * (2.0 / math.pi) + 0.5)
+    r = ((x - turns * 1.5703125) - turns * 4.8351287841796875e-4) - turns * 3.13855707645416259e-07
+    r2 = r * r
+    sine = r + r * r2 * (-1.6666654611e-1 + r2 * (8.3321608736e-3 + r2 * -1.9515295891e-4))
+    cosine = (1.0 - 0.5 * r2) + r2 * r2 * (
+        4.166664568298827e-2 + r2 * (-1.388731625493765e-3 + r2 * 2.443315711809948e-5)
+    )
+    quadrant = turns.astype(jnp.int32) & 3
+    odd = (quadrant & 1) == 1
+    first = jnp.where(odd, cosine, sine)
+    second = jnp.where(odd, sine, cosine)
+    sine = jnp.where(quadrant >= 2, -first, first)
+    cosine = jnp.where((quadrant == 1) | (quadrant == 2), -second, second)
+    return sine, cosine
 
 
 def fluxes(flow, area):
@@ -111,19 +128,31 @@
         load.start()
 
     loads[0].wait()
-    azimuth = angles[0:1, :]
-    elevation = angles[1:2, :]
-    cos_e = jnp.cos(elevation)
-    width = azimuth.shape[1]
+    width = angles.shape[1]
+    sine, cosine = sine_cosine(angles[...])
+    cos_e = cosine[1:2]
     places[me] = jnp.concatenate(
         [
-            SPHERE_RADIUS * (jnp.cos(azimuth) * cos_e),
-            SPHERE_RADIUS * (jnp.sin(azimuth) * cos_e),
-            SPHERE_RADIUS * jnp.sin(elevation),
+            SPHERE_RADIUS * (cosine[0:1] * cos_e),
+            SPHERE_RADIUS * (sine[0:1] * cos_e),
+            SPHERE_RADIUS * sine[1:2],
             jnp.zeros((5, width), F32),
         ],
         axis=0,
     )
+
+    neighbours = jnp.minimum(now, 1) + jnp.minimum(blocks - 1 - now, 1)
+    pl.semaphore_wait(barrier, groups - 1 + groups * neighbours)
+
+    def place_copy(i):
+        return pltpu.make_async_remote_copy(
+            src_ref=places.at[me], dst_ref=places.at[me],
+            send_sem=place_send.at[i], recv_sem=place_recv.at[me],
+            device_id=(order[i], now), device_id_type=MESH,
+        )
+
+    for i in range(1, groups):
+        place_copy(i).start()
 
     loads[1].wait()
     loads[2].wait()
@@ -137,16 +166,6 @@
         [flux[k, steps - 1 : steps, :] for k in range(4)] + [edge_pad], axis=0
     )
 
-    neighbours = jnp.minimum(now, 1) + jnp.minimum(blocks - 1 - now, 1)
-    pl.semaphore_wait(barrier, groups - 1 + groups * neighbours)
-
-    def place_copy(i):
-        return pltpu.make_async_remote_copy(
-            src_ref=places.at[me], dst_ref=places.at[me],
-            send_sem=place_send.at[i], recv_sem=place_recv.at[me],
-            device_id=(order[i], now), device_id_type=MESH,
-        )
-
     def edge_copy(side, block):
         return pltpu.make_async_remote_copy(
             src_ref=edge_out.at[side], dst_ref=edge_in.at[side],
@@ -154,9 +173,6 @@
             device_id=(me, block), device_id_type=MESH,
         )
 
-    for i in range(1, groups):
-        place_copy(i).start()
-
     @pl.when(has_before)
     def _():
         edge_copy(0, now - 1).start()
@@ -169,6 +185,11 @@
         for b in range(groups):
             landed[j, b, 0:steps, :] = jnp.zeros((steps, width), F32)
             landed[j, b, 2 * steps + TAIL :, :] = jnp.zeros((steps - TAIL, width), F32)
+
+    @pl.when(jnp.logical_not(has_before))
+    def _():
+        for b in range(groups):
+            landed[1, b, steps : 2 * steps + TAIL, :] = jnp.zeros((steps + TAIL, width), F32)
 
     loads[3].wait()
     loads[4].wait()
@@ -213,8 +234,10 @@
                 w_load[slot, load_rows, columns] = (tents[j] * by_load).astype(BF16)
 
     def part_copy(i, group, later):
+        count = steps + TAIL * later
         return pltpu.make_async_remote_copy(
-            src_ref=sent.at[group], dst_ref=landed.at[later, me, pl.ds(steps, steps + TAIL), :],
+            src_ref=sent.at[group, pl.ds(0, count), :],
+            dst_ref=landed.at[later, me, pl.ds(steps, count), :],
             send_sem=part_send.at[later, i], recv_sem=part_recv.at[later, me],
             device_id=(group, now + later), device_id_type=MESH,
         )
@@ -275,15 +298,17 @@
         if i > 0:
             part_copy(i, group, 0).start()
         else:
-            landed[0, me, steps : 2 * steps + TAIL, :] = total
+            landed[0, me, steps : 2 * steps, :] = total[:steps]
 
         @pl.when(has_after)
         def _():
             part_copy(i, group, 1).start()
 
     def arrived(later, block):
+        count = steps + TAIL * later
         return pltpu.make_async_remote_copy(
-            src_ref=sent.at[0], dst_ref=landed.at[later, block, pl.ds(steps, steps + TAIL), :],
+            src_ref=sent.at[0, pl.ds(0, count), :],
+            dst_ref=landed.at[later, block, pl.ds(steps, count), :],
             send_sem=part_send.at[later, 0], recv_sem=part_recv.at[later, block],
             device_id=(order[1], now), device_id_type=MESH,
         )
@@ -293,19 +318,14 @@
 
     @pl.when(has_before)
     def _():
-        for b in range(groups):
-            arrived(1, b).wait_recv()
-
-    @pl.when(jnp.logical_not(has_before))
-    def _():
-        for b in range(groups):
-            landed[1, b, steps : 2 * steps + TAIL, :] = jnp.zeros((steps + TAIL, width), F32)
+        for i in range(groups):
+            arrived(1, order[i]).wait_recv()
 
     result = jnp.zeros((steps, width), F32)
-    for b in range(groups):
-        offset = band[me, b]
-        result = result + landed[0, b, pl.ds(steps - offset, steps), :]
-        result = result + landed[1, b, pl.ds(2 * steps - offset, steps), :]
+    for block in range(groups):
+        offset = band[me, block]
+        result = result + landed[0, block, pl.ds(steps - offset, steps), :]
+        result = result + landed[1, block, pl.ds(2 * steps - offset, steps), :]
     out_ref[...] = result
 
     for i in range(1, groups):

time: 14.2 us -> 14.1 us (level)
  no operation moved by 1% of the time
where the time goes in v5:
time: 14.1 us; the launch traced here: 13.9 us
  Pallas kernels  13.3 us (94%)
  local copies, waits for them, and re-layouts  0.62 us (4%)
    pallas_call x1, Pallas kernels, local(): pl.pallas_call(functools.partial(kernel, groups, blocks), out_shape=jax.S...  13.3 us
    unnamed x1, local copies, waits for them, and re-layouts  0.62 us

profile of v5, /device:TPU:0, one launch (start us, length us, event | category | flops | bytes accessed | tf_op | source)
XLA Modules:
  0.0 13.9 jit_solution(18313085657051421248)
XLA Ops:
  0.0 13.3 %shard_map.55 = f32[64,128]{1,0:T(8,128)S(1)} custom-call(f32[5,64,512]{2,1,0:T(8,128)} %flow_hbm.1, f32[3,512]{1,0:T(4,128)} %pos_hbm.1, f32[3,512]{1,0:T(4,128)} %area_hbm.1, f32[2,128]{1,0:T(2,128)} %angles_hbm.1, s32[4,4]{1,0:T(4,128)} %band_hbm.1), custom_call_target="tpu_custom_call" | custom-call | tf_op jit(solution)/shard_map/pallas_call | solution.py:355
  13.3 0.6 %copy.7 = f32[64,128]{1,0:T(8,128)} copy(f32[64,128]{1,0:T(8,128)S(1)} %shard_map.55) | data formatting | bytes 65536

commit v6 on v5

--- a/solution.py
+++ b/solution.py
@@ -93,7 +93,8 @@
         side = groups
     high, low = me // side, lax.rem(me, side)
     shifts = [(i, j) for i in range(groups // side) for j in range(side)]
-    shifts.sort(key=lambda pair: (pair != (0, 0), -min(pair), -sum(pair)))
+    shifts.sort(key=lambda pair: (pair == (0, 0), -min(pair), -sum(pair)))
+    peers = range(groups - 1)
     order = [
         lax.rem(high + i, groups // side) * side + lax.rem(low + j, side) for i, j in shifts
     ]
@@ -105,18 +106,16 @@
     def greet(group, block):
         pl.semaphore_signal(barrier, inc=1, device_id=(group, block), device_id_type=MESH)
 
-    for i in range(1, groups):
+    for i in peers:
         greet(order[i], now)
 
     @pl.when(has_before)
     def _():
-        for i in range(groups):
-            greet(order[i], now - 1)
+        greet(me, now - 1)
 
     @pl.when(has_after)
     def _():
-        for i in range(groups):
-            greet(order[i], now + 1)
+        greet(me, now + 1)
 
     loads = [
         pltpu.make_async_copy(source, target, in_sem.at[i])
@@ -142,7 +141,7 @@
     )
 
     neighbours = jnp.minimum(now, 1) + jnp.minimum(blocks - 1 - now, 1)
-    pl.semaphore_wait(barrier, groups - 1 + groups * neighbours)
+    pl.semaphore_wait(barrier, groups - 1 + neighbours)
 
     def place_copy(i):
         return pltpu.make_async_remote_copy(
@@ -151,7 +150,7 @@
             device_id=(order[i], now), device_id_type=MESH,
         )
 
-    for i in range(1, groups):
+    for i in peers:
         place_copy(i).start()
 
     loads[1].wait()
@@ -249,7 +248,9 @@
             device_id=(order[i], now), device_id_type=MESH,
         ).wait_recv()
 
-    weigh(0, places[me][0:3])
+    if groups > 1:
+        await_places(0)
+    weigh(0, places[order[0]][0:3])
 
     @pl.when(has_before)
     def _():
@@ -281,7 +282,8 @@
         group = order[i]
         slot = i % 2
         if i + 1 < groups:
-            await_places(i + 1)
+            if i + 1 in peers:
+                await_places(i + 1)
             weigh(1 - slot, places[order[i + 1]][0:3])
         group_places = places[group][0:3]
         by_mass = jnp.dot(mass_rate[...], w_mass[slot], preferred_element_type=F32)
@@ -295,7 +297,7 @@
             piece = jnp.concatenate([piece, jnp.zeros((TAIL, width), F32)], axis=0)
             total = total + (pltpu.roll(piece, j, 0) if j else piece)
         sent[group] = total
-        if i > 0:
+        if i in peers:
             part_copy(i, group, 0).start()
         else:
             landed[0, me, steps : 2 * steps, :] = total[:steps]
@@ -310,10 +312,10 @@
             src_ref=sent.at[0, pl.ds(0, count), :],
             dst_ref=landed.at[later, block, pl.ds(steps, count), :],
             send_sem=part_send.at[later, 0], recv_sem=part_recv.at[later, block],
-            device_id=(order[1], now), device_id_type=MESH,
-        )
-
-    for i in range(1, groups):
+            device_id=(order[0], now), device_id_type=MESH,
+        )
+
+    for i in peers:
         arrived(0, order[i]).wait_recv()
 
     @pl.when(has_before)
@@ -328,7 +330,7 @@
         result = result + landed[1, block, pl.ds(2 * steps - offset, steps), :]
     out_ref[...] = result
 
-    for i in range(1, groups):
+    for i in peers:
         place_copy(i).wait_send()
         part_copy(i, order[i], 0).wait_send()
 

time: 14.1 us -> 13.7 us (0.972)
  Pallas kernels: 13.3 us -> 12.9 us
    pallas_call x1, Pallas kernels: 13.3 us -> 12.9 us  [local(): pl.pallas_call(functools.partial(kernel, groups, blocks), out_shape=jax.S...]
where the time goes in v6:
time: 13.7 us; the launch traced here: 13.5 us
  Pallas kernels  12.9 us (94%)
  local copies, waits for them, and re-layouts  0.62 us (5%)
    pallas_call x1, Pallas kernels, local(): pl.pallas_call(functools.partial(kernel, groups, blocks), out_shape=jax.S...  12.9 us
    unnamed x1, local copies, waits for them, and re-layouts  0.62 us

profile of v6, /device:TPU:0, one launch (start us, length us, event | category | flops | bytes accessed | tf_op | source)
XLA Modules:
  0.0 13.5 jit_solution(3438424842250391898)
XLA Ops:
  0.0 12.9 %shard_map.55 = f32[64,128]{1,0:T(8,128)S(1)} custom-call(f32[5,64,512]{2,1,0:T(8,128)} %flow_hbm.1, f32[3,512]{1,0:T(4,128)} %pos_hbm.1, f32[3,512]{1,0:T(4,128)} %area_hbm.1, f32[2,128]{1,0:T(2,128)} %angles_hbm.1, s32[4,4]{1,0:T(4,128)} %band_hbm.1), custom_call_target="tpu_custom_call" | custom-call | tf_op jit(solution)/shard_map/pallas_call | solution.py:357
  12.9 0.6 %copy.7 = f32[64,128]{1,0:T(8,128)} copy(f32[64,128]{1,0:T(8,128)S(1)} %shard_map.55) | data formatting | bytes 65536

commit v7 on v6

--- a/solution.py
+++ b/solution.py
@@ -17,7 +17,7 @@
 F32 = jnp.float32
 BF16 = jnp.bfloat16
 TAIL = 8
-CHUNK = 64
+CHUNK = 16
 
 
 def split3(x):
@@ -193,7 +193,7 @@
     loads[3].wait()
     loads[4].wait()
     spots = pos[...]
-    factors = jnp.transpose(point_factors(spots)).astype(BF16)
+    factors = point_factors(spots).astype(BF16)
     spot_rows = [spots[i : i + 1, :] for i in range(3)]
 
     def with_projection(parts):
@@ -208,12 +208,10 @@
     slope = NEAR_RANGE / SOUND_STEP
 
     def weigh(slot, group_places):
-        squared = jnp.dot(
-            factors, observer_factors(group_places).astype(BF16), preferred_element_type=F32
-        )
-        for start in range(0, points, CHUNK):
+        watchers = jnp.transpose(observer_factors(group_places)).astype(BF16)
+        squared = jnp.dot(watchers, factors, preferred_element_type=F32)
+        for start in range(0, width, CHUNK):
             rows = slice(start, start + CHUNK)
-            load_rows = slice(points + start, points + start + CHUNK)
             r = lax.rsqrt(squared[rows])
             u = near - slope * r
             z = u - r
@@ -227,10 +225,10 @@
             by_rate = r * (FOUR_PI / SOUND_STEP)
             by_load = r * r * (FOUR_PI * FOUR_PI)
             for j in range(LAGS):
-                columns = slice(j * width, (j + 1) * width)
-                w_mass[slot, rows, columns] = tents[j].astype(BF16)
-                w_load[slot, rows, columns] = (tents[j] * by_rate).astype(BF16)
-                w_load[slot, load_rows, columns] = (tents[j] * by_load).astype(BF16)
+                lag_rows = slice(j * width + start, j * width + start + CHUNK)
+                w_mass[slot, lag_rows, :] = tents[j].astype(BF16)
+                w_load[slot, lag_rows, :points] = (tents[j] * by_rate).astype(BF16)
+                w_load[slot, lag_rows, points:] = (tents[j] * by_load).astype(BF16)
 
     def part_copy(i, group, later):
         count = steps + TAIL * later
@@ -275,7 +273,8 @@
         later = jnp.where(row == steps - 1, edge_in[0, k : k + 1, :], pltpu.roll(mine, steps - 1, 0))
         earlier = jnp.where(row == 0, edge_in[1, k : k + 1, :], pltpu.roll(mine, 1, 0))
         rates.append(0.5 * (later - earlier))
-    mass_rate[...] = rates[0].astype(BF16)
+    mass_rate[:steps] = rates[0].astype(BF16)
+    mass_rate[steps:] = jnp.zeros((steps, points), BF16)
     steady_rate[:, :points] = with_projection(rates[1:])
 
     for i in range(groups):
@@ -285,17 +284,26 @@
             if i + 1 in peers:
                 await_places(i + 1)
             weigh(1 - slot, places[order[i + 1]][0:3])
-        group_places = places[group][0:3]
-        by_mass = jnp.dot(mass_rate[...], w_mass[slot], preferred_element_type=F32)
-        by_load = jnp.dot(steady_rate[...], w_load[slot], preferred_element_type=F32)
-        total = jnp.zeros((steps + TAIL, width), F32)
+        turned = jnp.transpose(places[group])
+        lane = lax.broadcasted_iota(jnp.int32, (width, 2 * steps), 1)
+        front = lane < steps
+        scale_low = jnp.where(front, turned[:, 0:1], turned[:, 1:2])
+        scale_high = jnp.where(front, turned[:, 2:3], 1.0)
+        across = (((1,), (1,)), ((), ()))
+        by_mass = lax.dot_general(
+            w_mass[slot], mass_rate[...], across, preferred_element_type=F32
+        )
+        by_load = lax.dot_general(
+            w_load[slot], steady_rate[...], across, preferred_element_type=F32
+        )
+        total = jnp.zeros((width, 2 * steps), F32)
         for j in range(LAGS):
-            columns = slice(j * width, (j + 1) * width)
-            piece = by_mass[:, columns] + by_load[3 * steps :, columns]
-            for k in range(3):
-                piece = piece + by_load[k * steps : (k + 1) * steps, columns] * group_places[k : k + 1]
-            piece = jnp.concatenate([piece, jnp.zeros((TAIL, width), F32)], axis=0)
-            total = total + (pltpu.roll(piece, j, 0) if j else piece)
+            rows = slice(j * width, (j + 1) * width)
+            piece = by_mass[rows] + by_load[rows, : 2 * steps] * scale_low
+            piece = piece + by_load[rows, 2 * steps :] * scale_high
+            piece = jnp.where(front, piece + pltpu.roll(piece, steps, 1), 0.0)
+            total = total + (pltpu.roll(piece, j, 1) if j else piece)
+        total = jnp.transpose(total)[: steps + TAIL]
         sent[group] = total
         if i in peers:
             part_copy(i, group, 0).start()
@@ -370,9 +378,9 @@
                 pltpu.VMEM((2, 8, points), F32),
                 pltpu.VMEM((4, steps, points), F32),
                 pltpu.VMEM((4 * steps, 2 * points), BF16),
-                pltpu.VMEM((steps, points), BF16),
-                pltpu.VMEM((2, points, LAGS * width), BF16),
-                pltpu.VMEM((2, 2 * points, LAGS * width), BF16),
+                pltpu.VMEM((2 * steps, points), BF16),
+                pltpu.VMEM((2, LAGS * width, points), BF16),
+                pltpu.VMEM((2, LAGS * width, 2 * points), BF16),
                 pltpu.VMEM((groups, steps + TAIL, width), F32),
                 pltpu.VMEM((2, groups, 3 * steps, width), F32),
                 dma((5,)),

time: 13.7 us -> 15.5 us (1.13)
  Pallas kernels: 12.9 us -> 14.8 us
    pallas_call x1, Pallas kernels: 12.9 us -> 14.8 us  [local(): pl.pallas_call(functools.partial(kernel, groups, blocks), out_shape=jax.S...]
where the time goes in v7:
time: 15.5 us; the launch traced here: 15.4 us
  Pallas kernels  14.8 us (95%)
  local copies, waits for them, and re-layouts  0.62 us (4%)
    pallas_call x1, Pallas kernels, local(): pl.pallas_call(functools.partial(kernel, groups, blocks), out_shape=jax.S...  14.8 us
    unnamed x1, local copies, waits for them, and re-layouts  0.62 us

profile of v7, /device:TPU:0, one launch (start us, length us, event | category | flops | bytes accessed | tf_op | source)
XLA Modules:
  0.0 15.4 jit_solution(1219170875840412315)
XLA Ops:
  0.0 14.8 %shard_map.55 = f32[64,128]{1,0:T(8,128)S(1)} custom-call(f32[5,64,512]{2,1,0:T(8,128)} %flow_hbm.1, f32[3,512]{1,0:T(4,128)} %pos_hbm.1, f32[3,512]{1,0:T(4,128)} %area_hbm.1, f32[2,128]{1,0:T(2,128)} %angles_hbm.1, s32[4,4]{1,0:T(4,128)} %band_hbm.1), custom_call_target="tpu_custom_call" | custom-call | tf_op jit(solution)/shard_map/pallas_call | solution.py:365
  14.8 0.6 %copy.7 = f32[64,128]{1,0:T(8,128)} copy(f32[64,128]{1,0:T(8,128)S(1)} %shard_map.55) | data formatting | bytes 65536

commit v8 on v6

--- a/solution.py
+++ b/solution.py
@@ -156,14 +156,11 @@
     loads[1].wait()
     loads[2].wait()
     area_rows = area[...]
-    whole = fluxes(flow, area_rows)
-    for k in range(4):
-        flux[k] = whole[k]
     edge_pad = jnp.zeros((4, points), F32)
-    edge_out[0] = jnp.concatenate([flux[k, 0:1, :] for k in range(4)] + [edge_pad], axis=0)
-    edge_out[1] = jnp.concatenate(
-        [flux[k, steps - 1 : steps, :] for k in range(4)] + [edge_pad], axis=0
-    )
+    first = fluxes(flow[:, 0:8, :], area_rows)
+    edge_out[0] = jnp.concatenate([part[0:1] for part in first] + [edge_pad], axis=0)
+    last = fluxes(flow[:, steps - 8 : steps, :], area_rows)
+    edge_out[1] = jnp.concatenate([part[7:8] for part in last] + [edge_pad], axis=0)
 
     def edge_copy(side, block):
         return pltpu.make_async_remote_copy(
@@ -179,6 +176,10 @@
     @pl.when(has_after)
     def _():
         edge_copy(1, now + 1).start()
+
+    whole = fluxes(flow, area_rows)
+    for k in range(4):
+        flux[k] = whole[k]
 
     for j in range(2):
         for b in range(groups):

time: 13.7 us -> 13.6 us (level)
  no operation moved by 1% of the time
where the time goes in v8:
time: 13.6 us; the launch traced here: 13.5 us
  Pallas kernels  12.8 us (94%)
  local copies, waits for them, and re-layouts  0.62 us (5%)
    pallas_call x1, Pallas kernels, local(): pl.pallas_call(functools.partial(kernel, groups, blocks), out_shape=jax.S...  12.8 us
    unnamed x1, local copies, waits for them, and re-layouts  0.62 us

profile of v8, /device:TPU:0, one launch (start us, length us, event | category | flops | bytes accessed | tf_op | source)
XLA Modules:
  0.0 13.5 jit_solution(11754442943035877622)
XLA Ops:
  0.0 12.8 %shard_map.55 = f32[64,128]{1,0:T(8,128)S(1)} custom-call(f32[5,64,512]{2,1,0:T(8,128)} %flow_hbm.1, f32[3,512]{1,0:T(4,128)} %pos_hbm.1, f32[3,512]{1,0:T(4,128)} %area_hbm.1, f32[2,128]{1,0:T(2,128)} %angles_hbm.1, s32[4,4]{1,0:T(4,128)} %band_hbm.1), custom_call_target="tpu_custom_call" | custom-call | tf_op jit(solution)/shard_map/pallas_call | solution.py:358
  12.8 0.6 %copy.7 = f32[64,128]{1,0:T(8,128)} copy(f32[64,128]{1,0:T(8,128)S(1)} %shard_map.55) | data formatting | bytes 65536
